TPU v7x, 512 devices: a whole 4x4x16 slice. The times are simulated.
512 devices in a mesh: dp: 32 (over z, core), fsdp: 16 (over x, y).
Axes of the slice: x: 4, y: 4, z: 16, core: 2. Of those that a mesh axis runs over, the one named last changes fastest.
Arguments:
- token_ids: int32 [65536], P(('dp', 'fsdp')), may hold values from 0 to 50431, as said below
- activations: bfloat16 [65536, 3072], P(('dp', 'fsdp'))
- grad_out: bfloat16 [65536, 3072], P(('dp', 'fsdp')), may hold values from -0.13183594 to 0.13183594
- error_buffer: bfloat16 [32, 3072, 3072], P('dp', 'fsdp'), may hold values from -6 to 6
- init_q: float32 [3072, 8], replicated, may hold values from -6 to 6
Outputs:
- p_factor: float32 [3072, 8], P('fsdp')
- q_factor: float32 [3072, 8], replicated
- error_next: bfloat16 [32, 3072, 3072], P('dp', 'fsdp')
Inputs may be any that keep to these rules, and one draw needn't show every extreme that they name: `token_ids`: id 1 is padding; on the rows of each device it forms a tail (possibly empty), and each device's first row holds id 0.
All inputs are finite; a program needn't handle non-finite values.
Results may differ from a plain program's by a relative error of at most 0.0006.
Values may be sent and summed in bfloat16 or wider, within the bound.
No kernel may reach another device: no remote copies, remote signals or barrier semaphores. Data moves between devices by JAX's collectives and lax.ppermute only.
A program may use at most 64 MiB of HBM per device.

v0:
```python
import jax
import jax.numpy as jnp
from jax import lax
from jax.sharding import PartitionSpec as P


def orthonormal_columns(p_rows):
    highest = lax.Precision.HIGHEST
    finished = []
    for index_col in range(p_rows.shape[1]):
        column = p_rows[:, index_col]
        if finished:
            stacked = jnp.stack(finished, axis=1)
            inner_vals = lax.psum(jnp.dot(column, stacked, precision=highest), "fsdp")
            column = column - jnp.dot(stacked, inner_vals, precision=highest)
        norm_square = lax.psum(jnp.sum(column * column), "fsdp")
        finished.append(column / jnp.sqrt(norm_square))
    return jnp.stack(finished, axis=1)


def on_device(token_ids, activations, grad_out, error_buffer, init_q):
    highest = lax.Precision.HIGHEST
    replicas = lax.axis_size("dp")
    valid_rows = (token_ids != 1).astype(grad_out.dtype)
    masked_grad = grad_out * valid_rows[:, None]
    x_cols = lax.all_to_all(activations, "fsdp", split_axis=1, concat_axis=0, tiled=True)
    error_rows = error_buffer[0]
    grad_rows = lax.dot_general(
        x_cols,
        lax.all_gather(masked_grad, "fsdp", axis=0, tiled=True),
        (((0,), (0,)), ((), ())),
        preferred_element_type=jnp.float32,
    )
    merged = grad_rows + error_rows.astype(jnp.float32)
    p_local = jnp.dot(merged, init_q, precision=highest)
    p_mean = lax.psum(p_local, "dp") / replicas
    ortho_basis = orthonormal_columns(p_mean)
    q_local = jnp.einsum(
        "rd,rk->dk", merged, ortho_basis, precision=highest, preferred_element_type=jnp.float32
    )
    q_factor = lax.psum(q_local, ("dp", "fsdp")) / replicas
    error_next = (merged - jnp.dot(ortho_basis, q_factor.T, precision=highest)).astype(jnp.bfloat16)
    return (ortho_basis, q_factor, error_next[None])


def solution(mesh):
    return jax.shard_map(
        on_device,
        mesh=mesh,
        in_specs=(
            P(("dp", "fsdp")),
            P(("dp", "fsdp"), None),
            P(("dp", "fsdp"), None),
            P("dp", "fsdp", None),
            P(),
        ),
        out_specs=(P("fsdp", None), P(), P("dp", "fsdp", None)),
        check_vma=False,
    )
```

profile of v0, /device:TPU:1, one launch (start us, length us, event | category | flops | bytes accessed | tf_op | source)
XLA Modules:
  0.0 1197.7 jit_solution(5980001329945168853)
XLA Ops:
  7.2 0.0 copy-start
  7.2 0.0 copy-start.1
  7.2 0.0 all-gather.2.cloned.1.call-start
  7.2 0.7 compare_convert_fusion
  8.0 2.1 broadcast_multiply_fusion
  10.1 0.0 all-gather.2.cloned.1.call-update
  10.1 0.0 all-reduce.2.cloned.1.call-start
  10.2 0.0 copy-done.1
  10.2 0.4 copy.8
  10.6 19.1 %all_to_all.19 = bf16[128,16,192]{0,2,1:T(8,128)(2,1)S(1)} all-to-all(bf16[128,16,192]{0,2,1:T(8,128)(2,1)S(1)} %bitcast.83), channel_id=1, replica_groups=mesh['dp'=32,'fsdp'=16] {'fsdp'}, dimensions={1} | all-to-all | bytes 1572864 | tf_op jit(solution)/shard_map/all_to_all | solution.py:26
  29.7 92.6 %all-gather.2.cloned.1.call-done = bf16[2048,3072]{1,0:T(8,128)(2,1)} async-done(((bf16[128,3072]{1,0:T(8,128)(2,1)}), bf16[2048,3072]{1,0:T(8,128)(2,1)}) %all-gather.2.cloned.1.call-update) | async-done | bytes 12582928 | tf_op jit(solution)/shard_map/all_gather | solution.py:30
  122.3 7.6 fusion
  129.9 0.0 copy-done
  130.0 1.9 fusion.29
  131.9 48.0 %psum.119 = f32[192,8]{0,1:T(8,128)S(1)} all-reduce(f32[192,8]{0,1:T(8,128)S(1)} %fusion.29), channel_id=1, replica_groups=mesh['dp'=32,'fsdp'=16] {'dp'}, use_global_device_ids=true, to_apply=%region_0.0 | all-reduce | flops 1536 | bytes 12288 | tf_op jit(solution)/shard_map/psum | solution.py:36
  179.9 0.6 multiply_reduce_fusion.8
  180.5 31.8 %psum.120 = f32[]{:T(128)} all-reduce(f32[]{:T(128)} %multiply_reduce_fusion.8), channel_id=1, replica_groups=mesh['dp'=32,'fsdp'=16] {'fsdp'}, use_global_device_ids=true, to_apply=%region_2.0 | all-reduce | flops 1 | bytes 8 | tf_op jit(solution)/shard_map/psum | solution.py:16
  213.0 0.6 multiply_reduce_fusion
  213.6 29.1 %psum.121 = f32[]{:T(128)} all-reduce(f32[]{:T(128)} %multiply_reduce_fusion), channel_id=1, replica_groups=mesh['dp'=32,'fsdp'=16] {'fsdp'}, use_global_device_ids=true, to_apply=%region_3.0 | all-reduce | flops 1 | bytes 8 | tf_op jit(solution)/shard_map/psum | solution.py:14
  242.8 1.2 multiply_reduce_fusion.7
  244.0 30.6 %psum.122 = f32[]{:T(128)} all-reduce(f32[]{:T(128)} %multiply_reduce_fusion.7), channel_id=1, replica_groups=mesh['dp'=32,'fsdp'=16] {'fsdp'}, use_global_device_ids=true, to_apply=%region_5.0 | all-reduce | flops 1 | bytes 8 | tf_op jit(solution)/shard_map/psum | solution.py:16
  275.3 0.7 broadcast_divide_fusion.6
  275.9 0.1 convolution_bitcast_fusion.6
  276.1 29.1 %psum.123 = f32[2]{0:T(128)S(1)} all-reduce(f32[2]{0:T(128)S(1)} %convolution_bitcast_fusion.6), channel_id=1, replica_groups=mesh['dp'=32,'fsdp'=16] {'fsdp'}, use_global_device_ids=true, to_apply=%region_6.0 | all-reduce | flops 2 | bytes 16 | tf_op jit(solution)/shard_map/psum | solution.py:14
  305.1 0.1 fusion.7
  305.3 0.6 multiply_reduce_fusion.6
  305.9 30.0 %psum.124 = f32[]{:T(128)} all-reduce(f32[]{:T(128)} %get-tuple-element.13), channel_id=1, replica_groups=mesh['dp'=32,'fsdp'=16] {'fsdp'}, use_global_device_ids=true, to_apply=%region_8.0 | all-reduce | flops 1 | bytes 8 | tf_op jit(solution)/shard_map/psum | solution.py:16
  336.6 0.1 convolution_bitcast_fusion.5
  336.7 29.1 %psum.125 = f32[3]{0:T(128)S(1)} all-reduce(f32[3]{0:T(128)S(1)} %convolution_bitcast_fusion.5), channel_id=1, replica_groups=mesh['dp'=32,'fsdp'=16] {'fsdp'}, use_global_device_ids=true, to_apply=%region_9.0 | all-reduce | flops 3 | bytes 24 | tf_op jit(solution)/shard_map/psum | solution.py:14
  365.8 0.1 fusion.5
  365.9 0.6 multiply_reduce_fusion.5
  366.5 30.0 %psum.126 = f32[]{:T(128)} all-reduce(f32[]{:T(128)} %get-tuple-element.11), channel_id=1, replica_groups=mesh['dp'=32,'fsdp'=16] {'fsdp'}, use_global_device_ids=true, to_apply=%region_11.0 | all-reduce | flops 1 | bytes 8 | tf_op jit(solution)/shard_map/psum | solution.py:16
  397.2 0.1 convolution_bitcast_fusion.4
  397.3 29.5 %psum.127 = f32[4]{0:T(128)S(1)} all-reduce(f32[4]{0:T(128)S(1)} %convolution_bitcast_fusion.4), channel_id=1, replica_groups=mesh['dp'=32,'fsdp'=16] {'fsdp'}, use_global_device_ids=true, to_apply=%region_12.0 | all-reduce | flops 4 | bytes 32 | tf_op jit(solution)/shard_map/psum | solution.py:14
  426.8 0.1 fusion.6
  427.0 0.6 multiply_reduce_fusion.4
  427.6 29.6 %psum.128 = f32[]{:T(128)} all-reduce(f32[]{:T(128)} %get-tuple-element.9), channel_id=1, replica_groups=mesh['dp'=32,'fsdp'=16] {'fsdp'}, use_global_device_ids=true, to_apply=%region_14.0 | all-reduce | flops 1 | bytes 8 | tf_op jit(solution)/shard_map/psum | solution.py:16
  457.9 0.1 convolution_bitcast_fusion.3
  458.0 29.8 %psum.129 = f32[5]{0:T(128)S(1)} all-reduce(f32[5]{0:T(128)S(1)} %convolution_bitcast_fusion.3), channel_id=1, replica_groups=mesh['dp'=32,'fsdp'=16] {'fsdp'}, use_global_device_ids=true, to_apply=%region_15.0 | all-reduce | flops 5 | bytes 40 | tf_op jit(solution)/shard_map/psum | solution.py:14
  487.8 0.1 fusion.12
  487.9 0.6 multiply_reduce_fusion.3
  488.5 29.3 %psum.130 = f32[]{:T(128)} all-reduce(f32[]{:T(128)} %get-tuple-element.7), channel_id=1, replica_groups=mesh['dp'=32,'fsdp'=16] {'fsdp'}, use_global_device_ids=true, to_apply=%region_17.0 | all-reduce | flops 1 | bytes 8 | tf_op jit(solution)/shard_map/psum | solution.py:16
  518.5 0.1 convolution_bitcast_fusion.2
  518.7 30.6 %psum.131 = f32[6]{0:T(128)S(1)} all-reduce(f32[6]{0:T(128)S(1)} %convolution_bitcast_fusion.2), channel_id=1, replica_groups=mesh['dp'=32,'fsdp'=16] {'fsdp'}, use_global_device_ids=true, to_apply=%region_18.0 | all-reduce | flops 6 | bytes 48 | tf_op jit(solution)/shard_map/psum | solution.py:14
  549.3 0.1 fusion.10
  549.4 0.6 multiply_reduce_fusion.2
  550.0 29.3 %psum.132 = f32[]{:T(128)} all-reduce(f32[]{:T(128)} %get-tuple-element.5), channel_id=1, replica_groups=mesh['dp'=32,'fsdp'=16] {'fsdp'}, use_global_device_ids=true, to_apply=%region_20.0 | all-reduce | flops 1 | bytes 8 | tf_op jit(solution)/shard_map/psum | solution.py:16
  580.1 0.1 convolution_bitcast_fusion.1
  580.2 30.5 %psum.133 = f32[7]{0:T(128)S(1)} all-reduce(f32[7]{0:T(128)S(1)} %convolution_bitcast_fusion.1), channel_id=1, replica_groups=mesh['dp'=32,'fsdp'=16] {'fsdp'}, use_global_device_ids=true, to_apply=%region_21.0 | all-reduce | flops 7 | bytes 56 | tf_op jit(solution)/shard_map/psum | solution.py:14
  610.7 0.1 fusion.8
  610.9 0.6 multiply_reduce_fusion.1
  611.5 29.1 %psum.134 = f32[]{:T(128)} all-reduce(f32[]{:T(128)} %get-tuple-element.3), channel_id=1, replica_groups=mesh['dp'=32,'fsdp'=16] {'fsdp'}, use_global_device_ids=true, to_apply=%region_23.0 | all-reduce | flops 1 | bytes 8 | tf_op jit(solution)/shard_map/psum | solution.py:16
  641.3 0.0 copy-start.3
  641.3 2.0 fusion.30
  643.3 0.0 all-reduce.2.cloned.1.call-update
  643.3 543.5 %all-reduce.2.cloned.1.call-done = f32[3072,8]{0,1:T(8,128)} async-done(((f32[3072,8]{0,1:T(8,128)}), f32[3072,8]{0,1:T(8,128)}) %all-reduce.2.cloned.1.call-update) | async-done | bytes 98320 | tf_op jit(solution)/shard_map/psum | solution.py:41
  1186.9 0.9 broadcast_multiply_fusion.1
  1187.8 0.0 copy-start.2
  1187.8 3.1 fusion.2
  1190.9 0.0 copy-done.3
  1190.9 0.0 copy-done.2
  (12 shorter events, 0.2 us)
Async XLA Ops:
  7.2 122.8 %copy-start = (f32[3072,8]{0,1:T(8,128)S(1)}, f32[3072,8]{0,1:T(8,128)}, u32[]{:S(2)}) copy-start(f32[3072,8]{0,1:T(8,128)} %param.9) | copy-start | bytes 294916
  7.2 3.0 copy-start.1
  7.2 115.1 %all-gather.2.cloned.1.call-start = ((), (), s32[]{:S(2)}) async-start(), calls=%async_computation.1 | async-start | bytes 13369344 | tf_op jit(solution)/shard_map/all_gather | solution.py:30
  10.1 1176.7 %all-reduce.2.cloned.1.call-start = ((), (), s32[]{:S(2)}) async-start(), calls=%async_computation.2 | async-start | bytes 196608 | tf_op jit(solution)/shard_map/psum | solution.py:41
  641.3 549.5 %copy-start.3 = (f32[192,8]{0,1:T(8,128)}, f32[192,8]{0,1:T(8,128)S(1)}, u32[]{:S(2)}) copy-start(f32[192,8]{0,1:T(8,128)S(1)} %stack.41) | copy-start | bytes 18436
  1187.8 3.1 copy-start.2
Sparse Core Ops, SparseCore 0:
  11.7 110.6 all-gather.1
  643.4 543.3 all-reduce.1
where the time goes:
time: 1200 us
  waiting for transfers between devices  636 us (53%)
  blocking collectives  514 us (43%)
  between operations  19.7 us (2%)
  matrix products  16.2 us (1%)
    psum x1, waiting for transfers between devices, on_device(): q_factor = lax.psum(q_local, ('dp', 'fsdp')) / replicas  544 us
    psum x8, blocking collectives, orthonormal_columns(): norm_square = lax.psum(jnp.sum(column * column), 'fsdp')  240 us
    psum x7, blocking collectives, orthonormal_columns(): inner_vals = lax.psum(jnp.dot(column, stacked, precision=highest), 'fsdp')  208 us
    all_gather x1, waiting for transfers between devices, on_device(): lax.all_gather(masked_grad, 'fsdp', axis=0, tiled=True)  92.6 us
    psum x1, blocking collectives, on_device(): p_mean = lax.psum(p_local, 'dp') / replicas  48 us
  transfers between devices with their start and end apart: 2, of which 2 were waited for; matrix products, arithmetic and copies ran while one was open for 0% of the time, Pallas kernels for 0%

commit v1 on v0

--- a/solution.py
+++ b/solution.py
@@ -38,7 +38,7 @@
     q_local = jnp.einsum(
         "rd,rk->dk", merged, ortho_basis, precision=highest, preferred_element_type=jnp.float32
     )
-    q_factor = lax.psum(q_local, ("dp", "fsdp")) / replicas
+    q_factor = lax.psum(lax.psum(q_local, "dp"), "fsdp") / replicas
     error_next = (merged - jnp.dot(ortho_basis, q_factor.T, precision=highest)).astype(jnp.bfloat16)
     return (ortho_basis, q_factor, error_next[None])
 

time: 1200 us -> 1050 us (0.88)
  waiting for transfers between devices: 636 us -> 492 us
    psum x1 -> x2, waiting for transfers between devices: 544 us -> 400 us  [on_device(): q_factor = lax.psum(lax.psum(q_local, 'dp'), 'fsdp') / replicas]
  transfers between devices with their start and end apart: 2 -> 3, of which waited for: 2 -> 3; matrix products, arithmetic and copies ran while one was open for 0% -> 0% of each run, Pallas kernels for 0% -> 0%
where the time goes in v1:
time: 1050 us
  blocking collectives  514 us (49%)
  waiting for transfers between devices  492 us (47%)
  between operations  19.4 us (2%)
  matrix products  16 us (2%)
  other arithmetic  10.6 us (1%)
    psum x2, waiting for transfers between devices, on_device(): q_factor = lax.psum(lax.psum(q_local, 'dp'), 'fsdp') / replicas  400 us
    psum x8, blocking collectives, orthonormal_columns(): norm_square = lax.psum(jnp.sum(column * column), 'fsdp')  240 us
    psum x7, blocking collectives, orthonormal_columns(): inner_vals = lax.psum(jnp.dot(column, stacked, precision=highest), 'fsdp')  208 us
    all_gather x1, waiting for transfers between devices, on_device(): lax.all_gather(masked_grad, 'fsdp', axis=0, tiled=True)  92.6 us
    psum x1, blocking collectives, on_device(): p_mean = lax.psum(p_local, 'dp') / replicas  48 us
  transfers between devices with their start and end apart: 3, of which 3 were waited for; matrix products, arithmetic and copies ran while one was open for 0% of the time, Pallas kernels for 0%

profile of v1, /device:TPU:1, one launch (start us, length us, event | category | flops | bytes accessed | tf_op | source)
XLA Modules:
  0.0 1053.4 jit_solution(7366049517486373123)
XLA Ops:
  7.2 0.0 copy-start
  7.2 0.0 copy-start.1
  7.2 0.0 all-gather.2.cloned.1.call-start
  7.2 0.7 compare_convert_fusion
  8.0 2.1 broadcast_multiply_fusion
  10.1 0.0 all-gather.2.cloned.1.call-update
  10.1 0.0 all-reduce.3.cloned.1.call-start
  10.2 0.0 copy-done.1
  10.2 0.4 copy.8
  10.6 19.1 %all_to_all.19 = bf16[128,16,192]{0,2,1:T(8,128)(2,1)S(1)} all-to-all(bf16[128,16,192]{0,2,1:T(8,128)(2,1)S(1)} %bitcast.83), channel_id=1, replica_groups=mesh['dp'=32,'fsdp'=16] {'fsdp'}, dimensions={1} | all-to-all | bytes 1572864 | tf_op jit(solution)/shard_map/all_to_all | solution.py:26
  29.7 92.6 %all-gather.2.cloned.1.call-done = bf16[2048,3072]{1,0:T(8,128)(2,1)} async-done(((bf16[128,3072]{1,0:T(8,128)(2,1)}), bf16[2048,3072]{1,0:T(8,128)(2,1)}) %all-gather.2.cloned.1.call-update) | async-done | bytes 12582928 | tf_op jit(solution)/shard_map/all_gather | solution.py:30
  122.3 7.5 fusion
  129.8 0.0 copy-done
  129.8 1.9 fusion.29
  131.7 48.0 %psum.126 = f32[192,8]{0,1:T(8,128)S(1)} all-reduce(f32[192,8]{0,1:T(8,128)S(1)} %fusion.29), channel_id=1, replica_groups=mesh['dp'=32,'fsdp'=16] {'dp'}, use_global_device_ids=true, to_apply=%region_0.0 | all-reduce | flops 1536 | bytes 12288 | tf_op jit(solution)/shard_map/psum | solution.py:36
  179.8 0.6 multiply_reduce_fusion.8
  180.4 31.8 %psum.127 = f32[]{:T(128)} all-reduce(f32[]{:T(128)} %multiply_reduce_fusion.8), channel_id=1, replica_groups=mesh['dp'=32,'fsdp'=16] {'fsdp'}, use_global_device_ids=true, to_apply=%region_2.0 | all-reduce | flops 1 | bytes 8 | tf_op jit(solution)/shard_map/psum | solution.py:16
  212.9 0.6 multiply_reduce_fusion
  213.5 29.1 %psum.128 = f32[]{:T(128)} all-reduce(f32[]{:T(128)} %multiply_reduce_fusion), channel_id=1, replica_groups=mesh['dp'=32,'fsdp'=16] {'fsdp'}, use_global_device_ids=true, to_apply=%region_3.0 | all-reduce | flops 1 | bytes 8 | tf_op jit(solution)/shard_map/psum | solution.py:14
  242.6 1.2 multiply_reduce_fusion.7
  243.8 30.6 %psum.129 = f32[]{:T(128)} all-reduce(f32[]{:T(128)} %multiply_reduce_fusion.7), channel_id=1, replica_groups=mesh['dp'=32,'fsdp'=16] {'fsdp'}, use_global_device_ids=true, to_apply=%region_5.0 | all-reduce | flops 1 | bytes 8 | tf_op jit(solution)/shard_map/psum | solution.py:16
  275.1 0.7 broadcast_divide_fusion.6
  275.8 0.1 convolution_bitcast_fusion.6
  275.9 29.1 %psum.130 = f32[2]{0:T(128)S(1)} all-reduce(f32[2]{0:T(128)S(1)} %convolution_bitcast_fusion.6), channel_id=1, replica_groups=mesh['dp'=32,'fsdp'=16] {'fsdp'}, use_global_device_ids=true, to_apply=%region_6.0 | all-reduce | flops 2 | bytes 16 | tf_op jit(solution)/shard_map/psum | solution.py:14
  305.0 0.1 fusion.7
  305.1 0.6 multiply_reduce_fusion.6
  305.7 30.0 %psum.131 = f32[]{:T(128)} all-reduce(f32[]{:T(128)} %get-tuple-element.13), channel_id=1, replica_groups=mesh['dp'=32,'fsdp'=16] {'fsdp'}, use_global_device_ids=true, to_apply=%region_8.0 | all-reduce | flops 1 | bytes 8 | tf_op jit(solution)/shard_map/psum | solution.py:16
  336.4 0.1 convolution_bitcast_fusion.5
  336.5 29.1 %psum.132 = f32[3]{0:T(128)S(1)} all-reduce(f32[3]{0:T(128)S(1)} %convolution_bitcast_fusion.5), channel_id=1, replica_groups=mesh['dp'=32,'fsdp'=16] {'fsdp'}, use_global_device_ids=true, to_apply=%region_9.0 | all-reduce | flops 3 | bytes 24 | tf_op jit(solution)/shard_map/psum | solution.py:14
  365.6 0.1 fusion.5
  365.8 0.6 multiply_reduce_fusion.5
  366.4 30.0 %psum.133 = f32[]{:T(128)} all-reduce(f32[]{:T(128)} %get-tuple-element.11), channel_id=1, replica_groups=mesh['dp'=32,'fsdp'=16] {'fsdp'}, use_global_device_ids=true, to_apply=%region_11.0 | all-reduce | flops 1 | bytes 8 | tf_op jit(solution)/shard_map/psum | solution.py:16
  397.0 0.1 convolution_bitcast_fusion.4
  397.2 29.5 %psum.134 = f32[4]{0:T(128)S(1)} all-reduce(f32[4]{0:T(128)S(1)} %convolution_bitcast_fusion.4), channel_id=1, replica_groups=mesh['dp'=32,'fsdp'=16] {'fsdp'}, use_global_device_ids=true, to_apply=%region_12.0 | all-reduce | flops 4 | bytes 32 | tf_op jit(solution)/shard_map/psum | solution.py:14
  426.7 0.1 fusion.6
  426.8 0.6 multiply_reduce_fusion.4
  427.4 29.6 %psum.135 = f32[]{:T(128)} all-reduce(f32[]{:T(128)} %get-tuple-element.9), channel_id=1, replica_groups=mesh['dp'=32,'fsdp'=16] {'fsdp'}, use_global_device_ids=true, to_apply=%region_14.0 | all-reduce | flops 1 | bytes 8 | tf_op jit(solution)/shard_map/psum | solution.py:16
  457.7 0.1 convolution_bitcast_fusion.3
  457.8 29.8 %psum.136 = f32[5]{0:T(128)S(1)} all-reduce(f32[5]{0:T(128)S(1)} %convolution_bitcast_fusion.3), channel_id=1, replica_groups=mesh['dp'=32,'fsdp'=16] {'fsdp'}, use_global_device_ids=true, to_apply=%region_15.0 | all-reduce | flops 5 | bytes 40 | tf_op jit(solution)/shard_map/psum | solution.py:14
  487.6 0.1 fusion.12
  487.8 0.6 multiply_reduce_fusion.3
  488.4 29.3 %psum.137 = f32[]{:T(128)} all-reduce(f32[]{:T(128)} %get-tuple-element.7), channel_id=1, replica_groups=mesh['dp'=32,'fsdp'=16] {'fsdp'}, use_global_device_ids=true, to_apply=%region_17.0 | all-reduce | flops 1 | bytes 8 | tf_op jit(solution)/shard_map/psum | solution.py:16
  518.4 0.1 convolution_bitcast_fusion.2
  518.5 30.6 %psum.138 = f32[6]{0:T(128)S(1)} all-reduce(f32[6]{0:T(128)S(1)} %convolution_bitcast_fusion.2), channel_id=1, replica_groups=mesh['dp'=32,'fsdp'=16] {'fsdp'}, use_global_device_ids=true, to_apply=%region_18.0 | all-reduce | flops 6 | bytes 48 | tf_op jit(solution)/shard_map/psum | solution.py:14
  549.1 0.1 fusion.10
  549.2 0.6 multiply_reduce_fusion.2
  549.9 29.3 %psum.139 = f32[]{:T(128)} all-reduce(f32[]{:T(128)} %get-tuple-element.5), channel_id=1, replica_groups=mesh['dp'=32,'fsdp'=16] {'fsdp'}, use_global_device_ids=true, to_apply=%region_20.0 | all-reduce | flops 1 | bytes 8 | tf_op jit(solution)/shard_map/psum | solution.py:16
  579.9 0.1 convolution_bitcast_fusion.1
  580.0 30.5 %psum.140 = f32[7]{0:T(128)S(1)} all-reduce(f32[7]{0:T(128)S(1)} %convolution_bitcast_fusion.1), channel_id=1, replica_groups=mesh['dp'=32,'fsdp'=16] {'fsdp'}, use_global_device_ids=true, to_apply=%region_21.0 | all-reduce | flops 7 | bytes 56 | tf_op jit(solution)/shard_map/psum | solution.py:14
  610.6 0.1 fusion.8
  610.7 0.6 multiply_reduce_fusion.1
  611.3 29.1 %psum.141 = f32[]{:T(128)} all-reduce(f32[]{:T(128)} %get-tuple-element.3), channel_id=1, replica_groups=mesh['dp'=32,'fsdp'=16] {'fsdp'}, use_global_device_ids=true, to_apply=%region_23.0 | all-reduce | flops 1 | bytes 8 | tf_op jit(solution)/shard_map/psum | solution.py:16
  641.2 0.0 copy-start.3
  641.2 2.0 fusion.30
  643.1 0.0 all-reduce.3.cloned.1.call-update
  643.2 0.0 all-reduce.5.cloned.1.call-start
  643.2 291.4 %all-reduce.3.cloned.1.call-done = f32[3072,8]{0,1:T(8,128)} async-done(((f32[3072,8]{0,1:T(8,128)}), f32[3072,8]{0,1:T(8,128)}) %all-reduce.3.cloned.1.call-update) | async-done | bytes 98320 | tf_op jit(solution)/shard_map/psum | solution.py:41
  934.6 0.0 all-reduce.5.cloned.1.call-update
  934.6 108.2 %all-reduce.5.cloned.1.call-done = f32[3072,8]{0,1:T(8,128)} async-done(((f32[3072,8]{0,1:T(8,128)}), f32[3072,8]{0,1:T(8,128)}) %all-reduce.5.cloned.1.call-update) | async-done | bytes 98320 | tf_op jit(solution)/shard_map/psum | solution.py:41
  1042.9 0.9 broadcast_multiply_fusion.1
  1043.8 0.0 copy-start.2
  1043.8 3.1 fusion.2
  1046.8 0.0 copy-done.3
  1046.9 0.0 copy-done.2
  (12 shorter events, 0.2 us)
Async XLA Ops:
  7.2 122.6 %copy-start = (f32[3072,8]{0,1:T(8,128)S(1)}, f32[3072,8]{0,1:T(8,128)}, u32[]{:S(2)}) copy-start(f32[3072,8]{0,1:T(8,128)} %param.9) | copy-start | bytes 294916
  7.2 3.0 copy-start.1
  7.2 115.1 %all-gather.2.cloned.1.call-start = ((), (), s32[]{:S(2)}) async-start(), calls=%async_computation.1 | async-start | bytes 13369344 | tf_op jit(solution)/shard_map/all_gather | solution.py:30
  10.1 924.5 %all-reduce.3.cloned.1.call-start = ((), (), s32[]{:S(2)}) async-start(), calls=%async_computation.2 | async-start | bytes 196608 | tf_op jit(solution)/shard_map/psum | solution.py:41
  641.2 405.7 %copy-start.3 = (f32[192,8]{0,1:T(8,128)}, f32[192,8]{0,1:T(8,128)S(1)}, u32[]{:S(2)}) copy-start(f32[192,8]{0,1:T(8,128)S(1)} %stack.41) | copy-start | bytes 18436
  643.2 399.7 %all-reduce.5.cloned.1.call-start = ((), (), s32[]{:S(2)}) async-start(), calls=%async_computation.3 | async-start | bytes 196608 | tf_op jit(solution)/shard_map/psum | solution.py:41
  1043.8 3.1 copy-start.2
Sparse Core Ops, SparseCore 0:
  11.7 110.6 all-gather.1
  643.3 291.2 all-reduce.2
  938.2 104.6 all-reduce.4
